TPU v7x, 1024 devices: a whole 4x8x16 slice. The times are simulated.
1024 devices in a mesh: row: 32 (over y_lo, z), col: 4 (over y_hi), depth: 8 (over x, core).
Axes of the slice: x: 4, y: 8 (y_hi: 4, y_lo: 2; y = y_hi * 2 + y_lo), z: 16, core: 2. Of those that a mesh axis runs over, the one named last changes fastest.
Arguments:
- tokens: bfloat16 [256, 8192], P('row', ('col', 'depth')), may hold values from -6 to 6
- grad_out: bfloat16 [256, 8192], P('row', ('col', 'depth')), may hold values from -6 to 6
- gate_weight: bfloat16 [8192, 28672], P(('col', 'depth'), 'row'), may hold values from -0.0625 to 0.0625
- up_weight: bfloat16 [8192, 28672], P(('col', 'depth'), 'row'), may hold values from -0.0625 to 0.0625
- down_weight: bfloat16 [28672, 8192], P('row', ('col', 'depth')), may hold values from -0.03125 to 0.03125
Outputs:
- layer_out: bfloat16 [256, 8192], P('row', ('col', 'depth'))
- grad_tokens: bfloat16 [256, 8192], P('row', ('col', 'depth'))
- grad_gate: bfloat16 [8192, 28672], P(('col', 'depth'), 'row')
- grad_up: bfloat16 [8192, 28672], P(('col', 'depth'), 'row')
- grad_down: bfloat16 [28672, 8192], P('row', ('col', 'depth'))
All inputs are finite; a program needn't handle non-finite values.
Results may differ from a plain program's by a relative error of at most 0.0049.
Values may be sent and summed in bfloat16 or wider, within the bound.
A program may use at most 32 MiB of HBM per device.

v0:
```python
import jax
import jax.numpy as jnp
from jax import lax
from jax.sharding import PartitionSpec as P


def contract_rows(left, right):
    return lax.dot_general(
        left, right, (((0,), (0,)), ((), ())), preferred_element_type=jnp.float32
    )


def contract_cols(left, right):
    return lax.dot_general(
        left, right, (((1,), (1,)), ((), ())), preferred_element_type=jnp.float32
    )


def gate_grads(d_hidden, gate_pre, up_proj):
    sigmoid_gate = jax.nn.sigmoid(gate_pre)
    d_gate = (d_hidden * up_proj * sigmoid_gate * (1.0 + gate_pre * (1.0 - sigmoid_gate))).astype(
        jnp.bfloat16
    )
    d_up = (d_hidden * gate_pre * sigmoid_gate).astype(jnp.bfloat16)
    return (d_gate, d_up)


def per_device(tokens, grad_out, gate_weight, up_weight, down_weight):
    width_ff = gate_weight.shape[1]
    own_rows = tokens.shape[0]
    tok_all, grad_all = (
        lax.all_gather(tokens, "row", axis=0, tiled=True),
        lax.all_gather(grad_out, "row", axis=0, tiled=True),
    )
    all_rows = tok_all.shape[0]
    share_rows = all_rows // lax.axis_size(("col", "depth"))
    w_both = jnp.concatenate([gate_weight, up_weight], axis=1)

    def ff_sums(term_fn):
        return lax.psum_scatter(
            term_fn(jnp.int32(0), share_rows * lax.axis_size(("col", "depth"))),
            ("col", "depth"),
            scatter_dimension=0,
            tiled=True,
        )

    def ff_panel(operand):
        return lax.all_gather(operand, ("col", "depth"), axis=0, tiled=True)

    def feature_sums(term_fn):
        return lax.psum_scatter(
            term_fn(jnp.int32(0), own_rows * lax.axis_size("row")),
            "row",
            scatter_dimension=0,
            tiled=True,
        )

    def gate_term(offset, length):
        return jnp.dot(tok_all, w_both, preferred_element_type=jnp.float32)

    gate_up = ff_sums(gate_term)
    gate_pre = gate_up[:, :width_ff]
    up_proj = gate_up[:, width_ff:]
    hidden = (gate_pre * jax.nn.sigmoid(gate_pre) * up_proj).astype(jnp.bfloat16)
    hid_all = ff_panel(hidden)

    def out_term(offset, length):
        return jnp.dot(hid_all, down_weight, preferred_element_type=jnp.float32)

    layer_out = feature_sums(out_term).astype(jnp.bfloat16)

    def back_term(offset, length):
        return contract_cols(grad_all, down_weight)

    d_hidden = ff_sums(back_term)
    d_gate, d_up = gate_grads(d_hidden, gate_pre, up_proj)
    d_all = ff_panel(jnp.concatenate([d_gate, d_up], axis=1))

    def input_term(offset, length):
        return contract_cols(d_all, w_both)

    grad_tokens = feature_sums(input_term).astype(jnp.bfloat16)
    grad_down = contract_rows(hid_all, grad_all).astype(jnp.bfloat16)
    grad_both = contract_rows(tok_all, d_all).astype(jnp.bfloat16)
    return (layer_out, grad_tokens, grad_both[:, :width_ff], grad_both[:, width_ff:], grad_down)


def solution(mesh):
    placed = (
        P("row", ("col", "depth")),
        P("row", ("col", "depth")),
        P(("col", "depth"), "row"),
        P(("col", "depth"), "row"),
        P("row", ("col", "depth")),
    )
    return jax.shard_map(
        per_device,
        mesh=mesh,
        in_specs=placed,
        out_specs=(
            P("row", ("col", "depth")),
            P("row", ("col", "depth")),
            P(("col", "depth"), "row"),
            P(("col", "depth"), "row"),
            P("row", ("col", "depth")),
        ),
        check_vma=False,
    )
```

profile of v0, /device:TPU:16, one launch (start us, length us, event | category | flops | bytes accessed | tf_op | source)
XLA Modules:
  0.0 820.3 jit_solution(8936106017456019639)
XLA Ops:
  7.3 76.7 %all_gather.14 = bf16[256,256]{1,0:T(8,128)(2,1)S(1)} all-gather(bf16[8,256]{1,0:T(8,128)(2,1)} %param.6), channel_id=1, replica_groups=mesh['row'=32,'col'=4,'depth'=8] {'row'}, dimensions={0}, use_global_device_ids=true | all-gather | bytes 135168 | tf_op jit(solution)/shard_map/all_gather | solution.py:33
  84.0 1.2 fusion.3
  85.3 59.1 %all_gather.12 = bf16[256,256]{1,0:T(8,128)(2,1)S(1)} all-gather(bf16[8,256]{1,0:T(8,128)(2,1)S(1)} %copy-done.3), channel_id=1, replica_groups=mesh['row'=32,'col'=4,'depth'=8] {'row'}, dimensions={0}, use_global_device_ids=true | all-gather | bytes 135168 | tf_op jit(solution)/shard_map/all_gather | solution.py:32
  144.6 0.5 convolution_bitcast_fusion
  145.0 1.7 copy.32
  146.8 1.3 dynamic-slice
  148.7 211.2 %all-reduce.3.cloned.1.call-done = f32[256,896]{0,1:T(8,128)} async-done(((f32[256,896]{0,1:T(8,128)}), f32[256,896]{0,1:T(8,128)}) %all-reduce.3.cloned.1.call-update) | async-done | bytes 917520
  359.9 1.2 constant_dynamic-slice_fusion
  361.1 0.1 copy.27
  361.3 132.7 %reduce-scatter.11.cloned.1.call-done = f32[8,1792]{1,0:T(8,128)} async-done(((f32[256,1792]{1,0:T(8,128)}), f32[8,1792]{1,0:T(8,128)}) %reduce-scatter.11.cloned.1.call-update) | async-done | bytes 57360 | tf_op jit(solution)/shard_map/reduce_scatter | solution.py:40
  494.0 0.8 multiply_convert_fusion.1
  494.8 40.4 %all_gather.15 = bf16[256,1792]{1,0:T(8,128)(2,1)S(1)} all-gather(bf16[8,1792]{1,0:T(8,128)(2,1)S(1)} %pad_maximum_fusion), channel_id=1, replica_groups=mesh['row'=32,'col'=4,'depth'=8] {'col','depth'}, dimensions={0}, use_global_device_ids=true | all-gather | bytes 946176 | tf_op jit(solution)/shard_map/all_gather | solution.py:48
  535.2 1.1 fusion.4
  536.4 39.5 %all_gather.13 = bf16[256,896]{1,0:T(8,128)(2,1)S(1)} all-gather(bf16[8,896]{1,0:T(8,128)(2,1)S(1)} %get-tuple-element.24), channel_id=1, replica_groups=mesh['row'=32,'col'=4,'depth'=8] {'col','depth'}, dimensions={0}, use_global_device_ids=true | all-gather | bytes 473088 | tf_op jit(solution)/shard_map/all_gather | solution.py:48
  575.9 1.0 fusion.2
  576.9 0.5 fusion
  577.4 0.1 fusion.1
  577.5 1.0 copy.29
  578.4 1.0 copy.30
  579.4 1.1 convolution_convert_fusion.1
  580.5 99.3 %reduce-scatter.9.cloned.1.call-done = f32[8,256]{1,0:T(8,128)} async-done(((f32[256,256]{1,0:T(8,128)}), f32[8,256]{1,0:T(8,128)}) %reduce-scatter.9.cloned.1.call-update) | async-done | bytes 8208 | tf_op jit(solution)/shard_map/reduce_scatter | solution.py:51
  679.8 1.3 convert_element_type.28
  681.1 131.4 %reduce-scatter.7.cloned.1.call-done = f32[8,256]{1,0:T(8,128)} async-done(((f32[256,256]{1,0:T(8,128)}), f32[8,256]{1,0:T(8,128)}) %reduce-scatter.7.cloned.1.call-update) | async-done | bytes 8208 | tf_op jit(solution)/shard_map/reduce_scatter | solution.py:51
  812.5 1.3 convert_element_type.25
  (19 shorter events, 0.3 us)
Async XLA Ops:
  7.2 76.8 %copy-start = (bf16[896,256]{1,0:T(8,128)(2,1)S(1)}, bf16[896,256]{1,0:T(8,128)(2,1)}, u32[]{:S(2)}) copy-start(bf16[896,256]{1,0:T(8,128)(2,1)} %param.9) | copy-start | bytes 1376260
  7.2 78.1 %copy-start.3 = (bf16[8,256]{1,0:T(8,128)(2,1)S(1)}, bf16[8,256]{1,0:T(8,128)(2,1)}, u32[]{:S(2)}) copy-start(bf16[8,256]{1,0:T(8,128)(2,1)} %param.5) | copy-start | bytes 12292
  7.2 137.3 %copy-start.1 = (bf16[256,896]{1,0:T(8,128)(2,1)S(1)}, bf16[256,896]{1,0:T(8,128)(2,1)}, u32[]{:S(2)}) copy-start(bf16[256,896]{1,0:T(8,128)(2,1)} %param.7) | copy-start | bytes 1376260
  7.2 137.3 %copy-start.2 = (bf16[256,896]{1,0:T(8,128)(2,1)S(1)}, bf16[256,896]{1,0:T(8,128)(2,1)}, u32[]{:S(2)}) copy-start(bf16[256,896]{1,0:T(8,128)(2,1)} %param.8) | copy-start | bytes 1376260
  7.2 352.7 %all-reduce.3.cloned.1.call-start = ((), (), s32[]{:S(2)}) async-start(), calls=%async_computation.6 | async-start | bytes 1835008
  85.3 408.7 %reduce-scatter.11.cloned.1.call-start = ((), (), s32[]{:S(2)}) async-start(), calls=%async_computation.5 | async-start | bytes 1892352 | tf_op jit(solution)/shard_map/reduce_scatter | solution.py:40
  146.8 533.0 %reduce-scatter.9.cloned.1.call-start = ((), (), s32[]{:S(2)}) async-start(), calls=%async_computation.4 | async-start | bytes 270336 | tf_op jit(solution)/shard_map/reduce_scatter | solution.py:51
  536.4 276.1 %reduce-scatter.7.cloned.1.call-start = ((), (), s32[]{:S(2)}) async-start(), calls=%async_computation.3 | async-start | bytes 270336 | tf_op jit(solution)/shard_map/reduce_scatter | solution.py:51
Sparse Core Ops, SparseCore 0:
  85.4 274.4 all-reduce.2
  366.5 127.4 reduce-scatter.10
  536.5 143.2 reduce-scatter.8
  683.0 129.4 reduce-scatter.6
where the time goes:
time: 821 us; the launch traced here: 820 us
  waiting for transfers between devices  575 us (70%)
  blocking collectives  216 us (26%)
  between operations  14.5 us (2%)
    reduce_scatter x2, waiting for transfers between devices, feature_sums(): lax.psum_scatter(term_fn(jnp.int32(0), own_rows * lax.axis_size('row')),...  231 us
    unnamed x5, waiting for transfers between devices  211 us
    reduce_scatter x1, waiting for transfers between devices, ff_sums(): lax.psum_scatter(term_fn(jnp.int32(0), share_rows * lax.axis_size(('col',...  133 us
    all_gather x2, blocking collectives, ff_panel(): return lax.all_gather(operand, ('col', 'depth'), axis=0, tiled=True)  79.9 us
    all_gather x1, blocking collectives, per_device(): lax.all_gather(grad_out, 'row', axis=0, tiled=True)  76.7 us
    all_gather x1, blocking collectives, per_device(): lax.all_gather(tokens, 'row', axis=0, tiled=True)  59.1 us
  transfers between devices with their start and end apart: 4, of which 4 were waited for; matrix products, arithmetic and copies ran while one was open for 1% of the time, Pallas kernels for 0%

commit v1 on v0

v1 whole, which is shorter than its diff:
```python
import jax
import jax.numpy as jnp
from jax import lax
from jax.experimental import pallas as pl
from jax.experimental.pallas import tpu as pltpu
from jax.sharding import PartitionSpec as P

MESH = pl.DeviceIdType.MESH
F32 = jnp.float32
BF16 = jnp.bfloat16
FAR_FIRST = (2, 1, 3, 0)


def dot(left, right, left_dim, right_dim):
    return lax.dot_general(
        left, right, (((left_dim,), (right_dim,)), ((), ())), preferred_element_type=F32
    )


def kernel(
    tok_ref, grad_ref, gw_hbm, uw_hbm, dw_hbm,
    lo_ref, gt_ref, gg_hbm, gu_hbm, gd_hbm,
    gw, uw, dw, gath, part, core_in, pack, plane_in, own, acts, p4, y_in, zpack, z_in, gg, gu, gd,
    load_sem, store_sem,
    tz_send, tz_recv, ty_send, ty_recv,
    pc_send, pc_recv, pp_send, pp_recv,
    ap_send, ap_recv, ac_send, ac_recv,
    oy_send, oy_recv, oz_send, oz_recv,
):
    row, col, depth = lax.axis_index("row"), lax.axis_index("col"), lax.axis_index("depth")
    y_lo, z = lax.div(row, 16), lax.rem(row, 16)
    x, core = lax.div(depth, 2), lax.rem(depth, 2)
    ff = gw.shape[1]
    d = gw.shape[0]

    def z_dev(other):
        return (y_lo * 16 + other, col, depth)

    y_dev = ((1 - y_lo) * 16 + z, col, depth)
    core_dev = (row, col, x * 2 + 1 - core)

    def plane_dev(other_col, other_x):
        return (row, other_col, other_x * 2 + core)

    def remote(src, dst, send, recv, device):
        return pltpu.make_async_remote_copy(
            src_ref=src, dst_ref=dst, send_sem=send, recv_sem=recv,
            device_id=device, device_id_type=MESH,
        )

    def z_off(i):
        return 8 + lax.div(i + 1, 2) * (2 * lax.rem(i, 2) - 1)

    loads = [
        pltpu.make_async_copy(gw_hbm, gw, load_sem.at[0]),
        pltpu.make_async_copy(uw_hbm, uw, load_sem.at[1]),
        pltpu.make_async_copy(dw_hbm, dw, load_sem.at[2]),
    ]
    for load in loads:
        load.start()

    barrier = pltpu.get_barrier_semaphore()

    def greet_z(i, c):
        pl.semaphore_signal(barrier, inc=1, device_id=z_dev(lax.rem(z + z_off(i), 16)), device_id_type=MESH)
        return c

    def greet_plane(i, c):
        pl.semaphore_signal(
            barrier, inc=1,
            device_id=plane_dev(lax.rem(col + lax.div(i, 4), 4), lax.rem(x + lax.rem(i, 4), 4)),
            device_id_type=MESH,
        )
        return c

    lax.fori_loop(0, 15, greet_z, 0)
    lax.fori_loop(1, 16, greet_plane, 0)
    pl.semaphore_signal(barrier, inc=1, device_id=y_dev, device_id_type=MESH)
    pl.semaphore_signal(barrier, inc=1, device_id=core_dev, device_id_type=MESH)
    gath[row] = jnp.concatenate(
        [tok_ref[...].astype(F32), grad_ref[...].astype(F32)], axis=0
    ).astype(BF16)
    pl.semaphore_wait(barrier, 32)

    def tz_copy(i):
        return remote(
            gath.at[row], gath.at[row], tz_send.at[i], tz_recv.at[z],
            z_dev(lax.rem(z + z_off(i), 16)),
        )

    def ty_copy(src_z):
        slot = y_lo * 16 + src_z
        return remote(gath.at[slot], gath.at[slot], ty_send.at[src_z], ty_recv.at[src_z], y_dev)

    def tz_start(i, c):
        tz_copy(i).start()
        return c

    lax.fori_loop(0, 15, tz_start, 0)
    ty_copy(z).start()

    def tz_pass(k, c):
        src_z = lax.rem(z + 16 - z_off(14 - k), 16)
        slot = y_lo * 16 + src_z
        remote(gath.at[slot], gath.at[slot], tz_send.at[0], tz_recv.at[src_z], y_dev).wait_recv()
        ty_copy(src_z).start()
        return c

    lax.fori_loop(0, 15, tz_pass, 0)

    def ty_arrive(src_z, c):
        slot = (1 - y_lo) * 16 + src_z
        remote(gath.at[slot], gath.at[slot], ty_send.at[src_z], ty_recv.at[src_z], y_dev).wait_recv()
        return c

    lax.fori_loop(0, 16, ty_arrive, 0)
    for load in loads:
        load.wait()

    both = gath[...].astype(F32)
    tok_all = both[:, :8, :].reshape(256, d).astype(BF16)
    grad_all = both[:, 8:, :].reshape(256, d).astype(BF16)

    part[:, :, :, 0:ff] = dot(tok_all, gw[...], 1, 0).reshape(16, 2, 8, ff)
    part[:, :, :, ff:2 * ff] = dot(tok_all, uw[...], 1, 0).reshape(16, 2, 8, ff)
    part[:, :, :, 2 * ff:] = dot(grad_all, dw[...], 1, 1).reshape(16, 2, 8, ff)

    def pc_copy(q):
        chips = pl.ds(lax.rem(col + q, 4) * 4, 4)
        return remote(part.at[chips, 1 - core], core_in.at[chips], pc_send.at[q], pc_recv.at[q], core_dev)

    for q in FAR_FIRST:
        pc_copy(q).start()

    me = col * 4 + x

    def pp_copy(q, step):
        other_col, other_x = lax.rem(col + q, 4), lax.rem(x + step, 4)
        return remote(
            pack.at[other_col * 4 + other_x], plane_in.at[me],
            pp_send.at[q * 4 + step], pp_recv.at[me], plane_dev(other_col, other_x),
        )

    for q in FAR_FIRST:
        pc_copy(q).wait_recv()
        chips = pl.ds(lax.rem(col + q, 4) * 4, 4)
        pack[chips] = (part[chips, core] + core_in[chips]).astype(BF16)
        for step in FAR_FIRST:
            if q or step:
                pp_copy(q, step).start()

    def pp_arrive(i, total):
        src = lax.rem(col + lax.div(i, 4), 4) * 4 + lax.rem(x + lax.rem(i, 4), 4)
        remote(plane_in.at[src], plane_in.at[src], pp_send.at[0], pp_recv.at[src], core_dev).wait_recv()
        return total + plane_in[src].astype(F32)

    total = lax.fori_loop(1, 16, pp_arrive, part[me, core] + core_in[me])

    gate_pre = total[:, 0:ff]
    up_proj = total[:, ff:2 * ff]
    d_hidden = total[:, 2 * ff:]
    sig = jax.nn.sigmoid(gate_pre)
    share = me * 2 + core
    acts[share, :, 0:ff] = (gate_pre * sig * up_proj).astype(BF16)
    acts[share, :, ff:2 * ff] = (
        d_hidden * up_proj * sig * (1.0 + gate_pre * (1.0 - sig))
    ).astype(BF16)
    acts[share, :, 2 * ff:] = (d_hidden * gate_pre * sig).astype(BF16)

    def ap_copy(i):
        other_col, other_x = lax.rem(col + lax.div(i, 4), 4), lax.rem(x + lax.rem(i, 4), 4)
        return remote(
            acts.at[share], acts.at[share], ap_send.at[i], ap_recv.at[me], plane_dev(other_col, other_x)
        )

    def ac_copy(chip):
        slot = chip * 2 + core
        return remote(acts.at[slot], acts.at[slot], ac_send.at[chip], ac_recv.at[chip], core_dev)

    for q in FAR_FIRST:
        for step in FAR_FIRST:
            if q or step:
                ap_copy(q * 4 + step).start()
    ac_copy(me).start()

    def ap_pass(q):
        def body(i, c):
            src = lax.rem(col + q, 4) * 4 + lax.rem(x + i, 4)
            slot = src * 2 + core
            remote(acts.at[slot], acts.at[slot], ap_send.at[0], ap_recv.at[src], core_dev).wait_recv()
            ac_copy(src).start()
            return c
        return body

    for q in (0, 1, 3, 2):
        lax.fori_loop(0 if q else 1, 4, ap_pass(q), 0)

    def ac_arrive(chip, c):
        slot = chip * 2 + 1 - core
        remote(acts.at[slot], acts.at[slot], ac_send.at[chip], ac_recv.at[chip], core_dev).wait_recv()
        return c

    lax.fori_loop(0, 16, ac_arrive, 0)

    hid = acts[:, :, 0:ff].astype(F32).reshape(256, ff).astype(BF16)
    d_gate = acts[:, :, ff:2 * ff].astype(F32).reshape(256, ff).astype(BF16)
    d_up = acts[:, :, 2 * ff:].astype(F32).reshape(256, ff).astype(BF16)

    p4[:, :, :, 0:d] = dot(hid, dw[...], 1, 0).reshape(2, 16, 8, d)
    p4[:, :, :, d:] = (dot(d_gate, gw[...], 1, 1) + dot(d_up, uw[...], 1, 1)).reshape(2, 16, 8, d)

    z_hi, z_sub = lax.div(z, 4), lax.rem(z, 4)

    def oy_copy(q):
        zs = pl.ds(lax.rem(z_hi + q, 4) * 4, 4)
        return remote(p4.at[1 - y_lo, zs], y_in.at[zs], oy_send.at[q], oy_recv.at[q], y_dev)

    for q in FAR_FIRST:
        oy_copy(q).start()

    gg[...] = dot(tok_all, d_gate, 0, 0).astype(BF16)
    stores = [pltpu.make_async_copy(gg, gg_hbm, store_sem.at[0])]
    stores[0].start()

    def oz_copy(q, step):
        other = lax.rem(z_hi + q, 4) * 4 + lax.rem(z_sub + step, 4)
        return remote(
            zpack.at[other], z_in.at[z], oz_send.at[q * 4 + step], oz_recv.at[z], z_dev(other)
        )

    for q in FAR_FIRST:
        oy_copy(q).wait_recv()
        zs = pl.ds(lax.rem(z_hi + q, 4) * 4, 4)
        zpack[zs] = (p4[y_lo, zs] + y_in[zs]).astype(BF16)
        for step in FAR_FIRST:
            if q or step:
                oz_copy(q, step).start()

    gu[...] = dot(tok_all, d_up, 0, 0).astype(BF16)
    stores.append(pltpu.make_async_copy(gu, gu_hbm, store_sem.at[1]))
    stores[1].start()
    gd[...] = dot(hid, grad_all, 0, 0).astype(BF16)
    stores.append(pltpu.make_async_copy(gd, gd_hbm, store_sem.at[2]))
    stores[2].start()

    def oz_arrive(i, total):
        src = lax.rem(z + i, 16)
        remote(z_in.at[src], z_in.at[src], oz_send.at[0], oz_recv.at[src], y_dev).wait_recv()
        return total + z_in[src].astype(F32)

    result = lax.fori_loop(1, 16, oz_arrive, p4[y_lo, z] + y_in[z])
    lo_ref[...] = result[:, 0:d].astype(BF16)
    gt_ref[...] = result[:, d:].astype(BF16)

    def tz_left(i, c):
        tz_copy(i).wait_send()
        return c

    def ty_left(i, c):
        ty_copy(i).wait_send()
        return c

    def ap_left(i, c):
        ap_copy(i).wait_send()
        return c

    def ac_left(i, c):
        ac_copy(i).wait_send()
        return c

    lax.fori_loop(0, 15, tz_left, 0)
    lax.fori_loop(0, 16, ty_left, 0)
    lax.fori_loop(1, 16, ap_left, 0)
    lax.fori_loop(0, 16, ac_left, 0)
    for q in FAR_FIRST:
        pc_copy(q).wait_send()
        oy_copy(q).wait_send()
        for step in FAR_FIRST:
            if q or step:
                pp_copy(q, step).wait_send()
                oz_copy(q, step).wait_send()
    for store in stores:
        store.wait()


def per_device(tokens, grad_out, gate_weight, up_weight, down_weight):
    d, ff = gate_weight.shape
    vmem = pl.BlockSpec(memory_space=pltpu.VMEM)
    hbm = pl.BlockSpec(memory_space=pl.ANY)
    dma = pltpu.SemaphoreType.DMA
    return pl.pallas_call(
        kernel,
        out_shape=(
            jax.ShapeDtypeStruct((8, d), BF16),
            jax.ShapeDtypeStruct((8, d), BF16),
            jax.ShapeDtypeStruct((d, ff), BF16),
            jax.ShapeDtypeStruct((d, ff), BF16),
            jax.ShapeDtypeStruct((ff, d), BF16),
        ),
        in_specs=[vmem, vmem, hbm, hbm, hbm],
        out_specs=(vmem, vmem, hbm, hbm, hbm),
        scratch_shapes=[
            pltpu.VMEM((d, ff), BF16),
            pltpu.VMEM((d, ff), BF16),
            pltpu.VMEM((ff, d), BF16),
            pltpu.VMEM((32, 16, d), BF16),
            pltpu.VMEM((16, 2, 8, 3 * ff), F32),
            pltpu.VMEM((16, 8, 3 * ff), F32),
            pltpu.VMEM((16, 8, 3 * ff), BF16),
            pltpu.VMEM((16, 8, 3 * ff), BF16),
            pltpu.VMEM((8, 3 * ff), F32),
            pltpu.VMEM((32, 8, 3 * ff), BF16),
            pltpu.VMEM((2, 16, 8, 2 * d), F32),
            pltpu.VMEM((16, 8, 2 * d), F32),
            pltpu.VMEM((16, 8, 2 * d), BF16),
            pltpu.VMEM((16, 8, 2 * d), BF16),
            pltpu.VMEM((d, ff), BF16),
            pltpu.VMEM((d, ff), BF16),
            pltpu.VMEM((ff, d), BF16),
            dma((3,)), dma((3,)),
            dma((15,)), dma((16,)), dma((16,)), dma((16,)),
            dma((4,)), dma((4,)), dma((16,)), dma((16,)),
            dma((16,)), dma((16,)), dma((16,)), dma((16,)),
            dma((4,)), dma((4,)), dma((16,)), dma((16,)),
        ],
        compiler_params=pltpu.CompilerParams(
            collective_id=0, has_side_effects=True, vmem_limit_bytes=44 << 20
        ),
        name="swiglu_exchange",
    )(tokens, grad_out, gate_weight, up_weight, down_weight)


def solution(mesh):
    acts = P("row", ("col", "depth"))
    weights = P(("col", "depth"), "row")
    return jax.shard_map(
        per_device,
        mesh=mesh,
        in_specs=(acts, acts, weights, weights, acts),
        out_specs=(acts, acts, weights, weights, acts),
        check_vma=False,
    )
```

time: 821 us -> 101 us (0.12)
  the two profiles are of different devices: /device:TPU:16 before, /device:TPU:1 now
where the time goes in v1:
time: 101 us
  Pallas kernels  92.2 us (91%)
  local copies, waits for them, and re-layouts  7.91 us (8%)
    pallas_call x1, Pallas kernels, per_device(): pl.pallas_call(kernel, out_shape=(jax.ShapeDtypeStruct((8, d), BF16), jax...  92.2 us
    unnamed x15, local copies, waits for them, and re-layouts  7.91 us

profile of v1, /device:TPU:1, one launch (start us, length us, event | category | flops | bytes accessed | tf_op | source)
XLA Modules:
  0.0 100.7 jit_solution(7181641478936979059)
XLA Ops:
  0.6 0.0 copy-start
  0.6 1.0 %copy-done = bf16[256,896]{1,0:T(8,128)(2,1)S(1)} copy-done((bf16[256,896]{1,0:T(8,128)(2,1)S(1)}, bf16[256,896]{1,0:T(8,128)(2,1)}, u32[]{:S(2)}) %copy-start) | copy-done | bytes 458776
  1.7 0.0 copy-start.1
  1.7 1.0 %copy-done.1 = bf16[256,896]{1,0:T(8,128)(2,1)S(1)} copy-done((bf16[256,896]{1,0:T(8,128)(2,1)S(1)}, bf16[256,896]{1,0:T(8,128)(2,1)}, u32[]{:S(2)}) %copy-start.1) | copy-done | bytes 458776
  2.7 0.0 copy-start.2
  2.7 1.0 %copy-done.2 = bf16[896,256]{1,0:T(8,128)(2,1)S(1)} copy-done((bf16[896,256]{1,0:T(8,128)(2,1)S(1)}, bf16[896,256]{1,0:T(8,128)(2,1)}, u32[]{:S(2)}) %copy-start.2) | copy-done | bytes 458776
  3.7 0.0 copy-start.3
  3.7 0.7 copy-done.3
  4.4 0.0 copy-start.4
  4.4 0.7 copy-done.4
  5.1 92.2 %swiglu_exchange.1 = (bf16[8,256]{1,0:T(8,128)(2,1)S(1)}, bf16[8,256]{1,0:T(8,128)(2,1)S(1)}, bf16[256,896]{1,0:T(8,128)(2,1)S(1)}, bf16[256,896]{1,0:T(8,128)(2,1)S(1)}, bf16[896,256]{1,0:T(8,128)(2,1)S(1)}) custom-call(bf16[8,256]{1,0:T(8,128)(2,1)S(1)} %copy-done.3, bf16[8,256]{1,0:T(8,128)(2,1)S(1)} %copy-done.4, bf16[256,896]{1,0:T(8,128)(2,1)S(1)} %copy-done, ...), custom_call_target="tpu_custom_call" | custom-call | tf_op jit(solution)/shard_map/swiglu_exchange/pallas_call | solution.py:291
  97.3 0.6 copy.15
  97.8 0.6 copy.16
  98.4 0.8 copy.17
  99.2 0.8 copy.18
  100.0 0.8 copy.19
Async XLA Ops:
  0.6 1.0 %copy-start = (bf16[256,896]{1,0:T(8,128)(2,1)S(1)}, bf16[256,896]{1,0:T(8,128)(2,1)}, u32[]{:S(2)}) copy-start(bf16[256,896]{1,0:T(8,128)(2,1)} %gw_hbm.1) | copy-start | bytes 1376260
  1.7 1.0 %copy-start.1 = (bf16[256,896]{1,0:T(8,128)(2,1)S(1)}, bf16[256,896]{1,0:T(8,128)(2,1)}, u32[]{:S(2)}) copy-start(bf16[256,896]{1,0:T(8,128)(2,1)} %uw_hbm.1) | copy-start | bytes 1376260
  2.7 1.0 %copy-start.2 = (bf16[896,256]{1,0:T(8,128)(2,1)S(1)}, bf16[896,256]{1,0:T(8,128)(2,1)}, u32[]{:S(2)}) copy-start(bf16[896,256]{1,0:T(8,128)(2,1)} %dw_hbm.1) | copy-start | bytes 1376260
  3.7 0.7 copy-start.3
  4.4 0.7 copy-start.4

commit v2 on v0

v2 whole, which is shorter than its diff:
```python
import functools
import jax
import jax.numpy as jnp
from jax import lax
from jax.experimental import pallas as pl
from jax.experimental.pallas import tpu as pltpu
from jax.sharding import PartitionSpec as P

MESH = pl.DeviceIdType.MESH
F32 = jnp.float32
BF16 = jnp.bfloat16
FAR = (2, 1, 3)
NEAR = (1, 3, 2)


def dot(left, right, left_dim, right_dim):
    return lax.dot_general(
        left, right, (((left_dim,), (right_dim,)), ((), ())), preferred_element_type=F32
    )


def kernel(
    tok_hbm, grad_hbm, gw_hbm, uw_hbm, dw_hbm,
    lo_ref, gt_ref, gg_hbm, gu_hbm, gd_hbm,
    gw, uw, dw, gath0, gath1,
    part0, part1, core_in0, core_in1, pack0, pack1, x_in0, x_in1, y_out0, y_out1, y_in0, y_in1,
    acts0, acts1, p4, n_in, zpack, z_in, gg, gu, gd,
    load_sem, store_sem,
    tz_send, tz_recv, ty_send, ty_recv,
    sc_send, sc_recv, sx_send, sx_recv, sy_send, sy_recv,
    ay_send, ay_recv, ax_send, ax_recv, ac_send, ac_recv,
    on_send, on_recv, oz_send, oz_recv,
):
    row, col, depth = lax.axis_index("row"), lax.axis_index("col"), lax.axis_index("depth")
    y_lo, z = lax.div(row, 16), lax.rem(row, 16)
    x, core = lax.div(depth, 2), lax.rem(depth, 2)
    d, ff = gw.shape
    gath = (gath0, gath1)
    part, core_in, pack = (part0, part1), (core_in0, core_in1), (pack0, pack1)
    x_in, y_out, y_in, acts = (x_in0, x_in1), (y_out0, y_out1), (y_in0, y_in1), (acts0, acts1)

    def z_dev(other):
        return (y_lo * 16 + other, col, depth)

    def col_dev(other):
        return (row, other, depth)

    def x_dev(other):
        return (row, col, other * 2 + core)

    next_dev = ((1 - y_lo) * 16 + z, col, depth)
    core_dev = (row, col, x * 2 + 1 - core)

    def remote(src, dst, send, recv, device):
        return pltpu.make_async_remote_copy(
            src_ref=src, dst_ref=dst, send_sem=send, recv_sem=recv,
            device_id=device, device_id_type=MESH,
        )

    def arrived(ref, recv):
        remote(ref, ref, load_sem.at[0], recv, core_dev).wait_recv()

    def left(ref, send):
        remote(ref, ref, send, load_sem.at[0], core_dev).wait_send()

    def z_off(i):
        return 8 + lax.div(i + 1, 2) * (2 * lax.rem(i, 2) - 1)

    def col_at(q):
        return lax.rem(col + q, 4)

    def x_at(step):
        return lax.rem(x + step, 4)

    own_loads = [
        pltpu.make_async_copy(tok_hbm, gath0.at[row], load_sem.at[0]),
        pltpu.make_async_copy(grad_hbm, gath1.at[row], load_sem.at[1]),
    ]
    loads = [
        pltpu.make_async_copy(gw_hbm, gw, load_sem.at[2]),
        pltpu.make_async_copy(uw_hbm, uw, load_sem.at[3]),
        pltpu.make_async_copy(dw_hbm, dw, load_sem.at[4]),
    ]
    for load in own_loads + loads:
        load.start()

    barrier = pltpu.get_barrier_semaphore()

    def greet(device):
        pl.semaphore_signal(barrier, inc=1, device_id=device, device_id_type=MESH)

    def greet_z(i, c):
        greet(z_dev(lax.rem(z + z_off(i), 16)))
        return c

    lax.fori_loop(0, 15, greet_z, 0)
    for step in FAR:
        greet(col_dev(col_at(step)))
        greet(x_dev(x_at(step)))
    greet(next_dev)
    greet(core_dev)
    for load in own_loads:
        load.wait()
    pl.semaphore_wait(barrier, 23)

    def pass_on(p, src_z):
        slot = gath[p].at[y_lo * 16 + src_z]
        remote(slot, slot, ty_send.at[p], ty_recv.at[p], next_dev).start()

    def gather_start(p):
        def body(i, c):
            slot = gath[p].at[row]
            remote(slot, slot, tz_send.at[p], tz_recv.at[p * 16 + z], z_dev(lax.rem(z + z_off(i), 16))).start()
            return c
        lax.fori_loop(0, 15, body, 0)
        pass_on(p, z)

    def gather_pass(p):
        def body(k, c):
            src_z = lax.rem(z + 16 - z_off(14 - k), 16)
            arrived(gath[p].at[y_lo * 16 + src_z], tz_recv.at[p * 16 + src_z])
            pass_on(p, src_z)
            return c
        lax.fori_loop(0, 15, body, 0)

    def gather_all(p):
        arrived(gath[p].at[pl.ds((1 - y_lo) * 16, 16)], ty_recv.at[p])
        return gath[p][...].astype(F32).reshape(256, d).astype(BF16)

    def sums_start(p):
        for q in FAR + (0,):
            chips = pl.ds(col_at(q) * 4, 4)
            remote(
                part[p].at[chips, 1 - core], core_in[p].at[chips],
                sc_send.at[p], sc_recv.at[p * 4 + q], core_dev,
            ).start()

    def sums_x(p, q):
        first = col_at(q) * 4
        chips = pl.ds(first, 4)
        arrived(core_in[p].at[chips], sc_recv.at[p * 4 + q])
        pack[p][chips] = (part[p][chips, core] + core_in[p][chips]).astype(BF16)
        for step in FAR:
            remote(
                pack[p].at[first + x_at(step)], x_in[p].at[first + x],
                sx_send.at[p], sx_recv.at[p * 4 + col_at(q)], x_dev(x_at(step)),
            ).start()

    def sums_y(p, q):
        first = col_at(q) * 4
        arrived(x_in[p].at[pl.ds(0, 3)], sx_recv.at[p * 4 + col_at(q)])
        total = part[p][first + x, core] + core_in[p][first + x]
        for step in FAR:
            total = total + x_in[p][first + x_at(step)].astype(F32)
        y_out[p][col_at(q)] = total
        if q:
            remote(
                y_out[p].at[col_at(q)], y_in[p].at[col], sy_send.at[p], sy_recv.at[p], col_dev(col_at(q))
            ).start()

    def sums_total(p):
        arrived(y_in[p].at[pl.ds(0, 3)], sy_recv.at[p])
        total = y_out[p][col]
        for q in FAR:
            total = total + y_in[p][col_at(q)]
        return total

    def acts_x(p, q):
        slot = acts[p].at[col_at(q) * 4 + x, core]
        for step in FAR:
            remote(
                slot, slot, ax_send.at[p], ax_recv.at[p * 4 + col_at(q)], x_dev(x_at(step))
            ).start()

    def acts_start(p):
        slot = acts[p].at[col * 4 + x, core]
        for q in FAR:
            remote(slot, slot, ay_send.at[p], ay_recv.at[p * 4 + col], col_dev(col_at(q))).start()
        acts_x(p, 0)

    def acts_y(p, q):
        arrived(acts[p].at[col_at(q) * 4 + x, core], ay_recv.at[p * 4 + col_at(q)])
        acts_x(p, q)

    def acts_core(p, q):
        arrived(acts[p].at[pl.ds(0, 3), core], ax_recv.at[p * 4 + col_at(q)])
        group = acts[p].at[pl.ds(col_at(q) * 4, 4), core]
        remote(group, group, ac_send.at[p], ac_recv.at[p], core_dev).start()

    def acts_all(p):
        arrived(acts[p].at[:, core], ac_recv.at[p])

    z_hi, z_sub = lax.div(z, 4), lax.rem(z, 4)

    def out_start(p):
        for q in FAR + (0,):
            zs = pl.ds(lax.rem(z_hi + q, 4) * 4, 4)
            remote(
                p4.at[p, 1 - y_lo, zs], n_in.at[p, zs], on_send.at[p], on_recv.at[p * 4 + q], next_dev
            ).start()

    def out_z(p, q):
        first = lax.rem(z_hi + q, 4) * 4
        zs = pl.ds(first, 4)
        arrived(n_in.at[p, zs], on_recv.at[p * 4 + q])
        zpack[p, zs] = (p4[p, y_lo, zs] + n_in[p, zs]).astype(BF16)
        for step in FAR + (0,):
            if q or step:
                other = first + lax.rem(z_sub + step, 4)
                remote(
                    zpack.at[p, other], z_in.at[p, z], oz_send.at[p], oz_recv.at[p], z_dev(other)
                ).start()

    def out_all(p):
        arrived(z_in.at[p, pl.ds(0, 15)], oz_recv.at[p])
        total = p4[p, y_lo, z] + n_in[p, z]

        def body(i, total):
            return total + z_in[p, lax.rem(z + i, 16)].astype(F32)

        return lax.fori_loop(1, 16, body, total).astype(BF16)

    gather_start(0)
    gather_start(1)
    gather_pass(0)
    tok_all = gather_all(0)
    for load in loads:
        load.wait()
    part0[:, :, :, 0:ff] = dot(tok_all, gw[...], 1, 0).reshape(16, 2, 8, ff)
    part0[:, :, :, ff:] = dot(tok_all, uw[...], 1, 0).reshape(16, 2, 8, ff)
    sums_start(0)
    gather_pass(1)
    for q in FAR + (0,):
        sums_x(0, q)
    grad_all = gather_all(1)
    part1[...] = dot(grad_all, dw[...], 1, 1).reshape(16, 2, 8, ff)
    sums_start(1)
    for q in FAR:
        sums_y(0, q)
    for q in FAR + (0,):
        sums_x(1, q)
    sums_y(0, 0)
    total = sums_total(0)
    gate_pre = total[:, 0:ff]
    up_proj = total[:, ff:]
    sig = jax.nn.sigmoid(gate_pre)
    acts0[col * 4 + x, core] = (gate_pre * sig * up_proj).astype(BF16)
    acts_start(0)
    for q in FAR + (0,):
        sums_y(1, q)
    for q in NEAR:
        acts_y(0, q)
    d_hidden = sums_total(1)
    acts1[col * 4 + x, core, :, 0:ff] = (
        d_hidden * up_proj * sig * (1.0 + gate_pre * (1.0 - sig))
    ).astype(BF16)
    acts1[col * 4 + x, core, :, ff:] = (d_hidden * gate_pre * sig).astype(BF16)
    acts_start(1)
    for q in (0,) + NEAR:
        acts_core(0, q)
    for q in NEAR:
        acts_y(1, q)
    acts_all(0)
    hid = acts0[...].astype(F32).reshape(256, ff).astype(BF16)
    p4[0] = dot(hid, dw[...], 1, 0).reshape(2, 16, 8, d)
    out_start(0)
    for q in (0,) + NEAR:
        acts_core(1, q)
    for q in FAR + (0,):
        out_z(0, q)
    acts_all(1)
    d_gate = acts1[:, :, :, 0:ff].astype(F32).reshape(256, ff).astype(BF16)
    d_up = acts1[:, :, :, ff:].astype(F32).reshape(256, ff).astype(BF16)
    p4[1] = (dot(d_gate, gw[...], 1, 1) + dot(d_up, uw[...], 1, 1)).reshape(2, 16, 8, d)
    out_start(1)
    gg[...] = dot(tok_all, d_gate, 0, 0).astype(BF16)
    stores = [pltpu.make_async_copy(gg, gg_hbm, store_sem.at[0])]
    stores[0].start()
    for q in FAR + (0,):
        out_z(1, q)
    gu[...] = dot(tok_all, d_up, 0, 0).astype(BF16)
    stores.append(pltpu.make_async_copy(gu, gu_hbm, store_sem.at[1]))
    stores[1].start()
    gd[...] = dot(hid, grad_all, 0, 0).astype(BF16)
    stores.append(pltpu.make_async_copy(gd, gd_hbm, store_sem.at[2]))
    stores[2].start()
    for p in (0, 1):
        left(gath[p].at[pl.ds(0, 15)], tz_send.at[p])
        left(gath[p].at[pl.ds(0, 16)], ty_send.at[p])
        left(core_in[p], sc_send.at[p])
        left(pack[p].at[pl.ds(0, 12)], sx_send.at[p])
        left(y_in[p].at[pl.ds(0, 3)], sy_send.at[p])
        left(acts[p].at[pl.ds(0, 3), core], ay_send.at[p])
        left(acts[p].at[pl.ds(0, 12), core], ax_send.at[p])
        left(acts[p].at[:, core], ac_send.at[p])
        left(n_in.at[p], on_send.at[p])
    lo_ref[...] = out_all(0)
    gt_ref[...] = out_all(1)
    for p in (0, 1):
        left(zpack.at[p, pl.ds(0, 15)], oz_send.at[p])
    for store in stores:
        store.wait()


def land(*refs):
    sources, targets, sem = refs[:5], refs[5:10], refs[10]
    copies = [
        pltpu.make_async_copy(source, target, sem.at[i])
        for i, (source, target) in enumerate(zip(sources, targets))
    ]
    for copy in copies:
        copy.start()
    for copy in copies:
        copy.wait()


def per_device(tokens, grad_out, gate_weight, up_weight, down_weight):
    d, ff = gate_weight.shape
    vmem = pl.BlockSpec(memory_space=pltpu.VMEM)
    hbm = pl.BlockSpec(memory_space=pltpu.HBM)
    dma = pltpu.SemaphoreType.DMA
    pair = (1, 1)
    results = pl.pallas_call(
        kernel,
        out_shape=(
            jax.ShapeDtypeStruct((8, d), BF16),
            jax.ShapeDtypeStruct((8, d), BF16),
            jax.ShapeDtypeStruct((d, ff), BF16),
            jax.ShapeDtypeStruct((d, ff), BF16),
            jax.ShapeDtypeStruct((ff, d), BF16),
        ),
        in_specs=[hbm] * 5,
        out_specs=(vmem, vmem, hbm, hbm, hbm),
        scratch_shapes=[
            pltpu.VMEM((d, ff), BF16),
            pltpu.VMEM((d, ff), BF16),
            pltpu.VMEM((ff, d), BF16),
            pltpu.VMEM((32, 8, d), BF16),
            pltpu.VMEM((32, 8, d), BF16),
            pltpu.VMEM((16, 2, 8, 2 * ff), F32),
            pltpu.VMEM((16, 2, 8, ff), F32),
            pltpu.VMEM((16, 8, 2 * ff), F32),
            pltpu.VMEM((16, 8, ff), F32),
            pltpu.VMEM((16, 8, 2 * ff), BF16),
            pltpu.VMEM((16, 8, ff), BF16),
            pltpu.VMEM((16, 8, 2 * ff), BF16),
            pltpu.VMEM((16, 8, ff), BF16),
            pltpu.VMEM((4, 8, 2 * ff), F32),
            pltpu.VMEM((4, 8, ff), F32),
            pltpu.VMEM((4, 8, 2 * ff), F32),
            pltpu.VMEM((4, 8, ff), F32),
            pltpu.VMEM((16, 2, 8, ff), BF16),
            pltpu.VMEM((16, 2, 8, 2 * ff), BF16),
            pltpu.VMEM((2, 2, 16, 8, d), F32),
            pltpu.VMEM((2, 16, 8, d), F32),
            pltpu.VMEM((2, 16, 8, d), BF16),
            pltpu.VMEM((2, 16, 8, d), BF16),
            pltpu.VMEM((d, ff), BF16),
            pltpu.VMEM((d, ff), BF16),
            pltpu.VMEM((ff, d), BF16),
            dma((5,)), dma((3,)),
            dma((2,)), dma((32,)), dma((2,)), dma((2,)),
            dma((2,)), dma((8,)), dma((2,)), dma((8,)), dma((2,)), dma((2,)),
            dma((2,)), dma((8,)), dma((2,)), dma((8,)), dma((2,)), dma((2,)),
            dma((2,)), dma((8,)), dma((2,)), dma((2,)),
        ],
        compiler_params=pltpu.CompilerParams(
            collective_id=0, has_side_effects=True, vmem_limit_bytes=62 << 20
        ),
        name="swiglu_exchange",
    )(tokens, grad_out, gate_weight, up_weight, down_weight)
    return pl.pallas_call(
        land,
        out_shape=tuple(jax.ShapeDtypeStruct(r.shape, r.dtype) for r in results),
        in_specs=[pl.BlockSpec(memory_space=pl.ANY)] * 5,
        out_specs=(pl.BlockSpec(memory_space=pl.ANY),) * 5,
        scratch_shapes=[dma((5,))],
        name="land",
    )(*results)


def solution(mesh):
    acts = P("row", ("col", "depth"))
    weights = P(("col", "depth"), "row")
    return jax.shard_map(
        per_device,
        mesh=mesh,
        in_specs=(acts, acts, weights, weights, acts),
        out_specs=(acts, acts, weights, weights, acts),
        check_vma=False,
    )
```

time: 821 us -> 121 us (0.15)
  the two profiles are of different devices: /device:TPU:16 before, /device:TPU:1 now
where the time goes in v2:
time: 121 us
  Pallas kernels  120 us (99%)
    pallas_call x1, Pallas kernels, per_device(): pl.pallas_call(kernel, out_shape=(jax.ShapeDtypeStruct((8, d), BF16), jax...  77.4 us
    pallas_call x1, Pallas kernels, per_device(): pl.pallas_call(land, out_shape=tuple((jax.ShapeDtypeStruct(r.shape, r.dty...  43.1 us

profile of v2, /device:TPU:1, one launch (start us, length us, event | category | flops | bytes accessed | tf_op | source)
XLA Modules:
  0.0 121.1 jit_solution(5160694243225706058)
XLA Ops:
  0.6 77.4 %swiglu_exchange.1 = (bf16[8,256]{1,0:T(8,128)(2,1)}, bf16[8,256]{1,0:T(8,128)(2,1)}, bf16[256,896]{1,0:T(8,128)(2,1)}, bf16[256,896]{1,0:T(8,128)(2,1)}, bf16[896,256]{1,0:T(8,128)(2,1)}) custom-call(bf16[8,256]{1,0:T(8,128)(2,1)} %tok_hbm.1, bf16[8,256]{1,0:T(8,128)(2,1)} %grad_hbm.1, bf16[256,896]{1,0:T(8,128)(2,1)} %gw_hbm.1, bf16[256,896]{1,0:T(8,128)(2,1)} %uw_hbm.1, ...), custom_call_target="tpu_custom_call" | custom-call | tf_op jit(solution)/shard_map/swiglu_exchange/pallas_call | solution.py:323
  78.0 43.1 %land.1 = (bf16[8,256]{1,0:T(8,128)(2,1)}, bf16[8,256]{1,0:T(8,128)(2,1)}, bf16[256,896]{1,0:T(8,128)(2,1)}, bf16[256,896]{1,0:T(8,128)(2,1)}, bf16[896,256]{1,0:T(8,128)(2,1)}) custom-call(bf16[8,256]{1,0:T(8,128)(2,1)} %get-tuple-element.10.refs_0_, bf16[8,256]{1,0:T(8,128)(2,1)} %get-tuple-element.11.refs_1_, bf16[256,896]{1,0:T(8,128)(2,1)} %get-tuple-element.12.refs_2_, ...), custom_call_target="tpu_custom_call" | custom-call | tf_op jit(solution)/shard_map/land/pallas_call | solution.py:372

commit v3 on v2

--- a/solution.py
+++ b/solution.py
@@ -303,15 +303,23 @@
 
 
 def land(*refs):
-    sources, targets, sem = refs[:5], refs[5:10], refs[10]
-    copies = [
-        pltpu.make_async_copy(source, target, sem.at[i])
-        for i, (source, target) in enumerate(zip(sources, targets))
+    sources, targets, held = refs[:5], refs[5:10], refs[10:15]
+    in_sem, out_sem = refs[15:]
+    loads = [
+        pltpu.make_async_copy(source, buf, in_sem.at[i])
+        for i, (source, buf) in enumerate(zip(sources, held))
     ]
-    for copy in copies:
-        copy.start()
-    for copy in copies:
-        copy.wait()
+    stores = [
+        pltpu.make_async_copy(buf, target, out_sem.at[i])
+        for i, (buf, target) in enumerate(zip(held, targets))
+    ]
+    for load in loads:
+        load.start()
+    for load, store in zip(loads, stores):
+        load.wait()
+        store.start()
+    for store in stores:
+        store.wait()
 
 
 def per_device(tokens, grad_out, gate_weight, up_weight, down_weight):
@@ -374,7 +382,7 @@
         out_shape=tuple(jax.ShapeDtypeStruct(r.shape, r.dtype) for r in results),
         in_specs=[pl.BlockSpec(memory_space=pl.ANY)] * 5,
         out_specs=(pl.BlockSpec(memory_space=pl.ANY),) * 5,
-        scratch_shapes=[dma((5,))],
+        scratch_shapes=[pltpu.VMEM(r.shape, r.dtype) for r in results] + [dma((5,)), dma((5,))],
         name="land",
     )(*results)
 

time: 121 us -> 80.4 us (0.66)
  Pallas kernels: 120 us -> 79.6 us
    pallas_call x1, Pallas kernels: 43.1 us -> 2.18 us  [per_device(): pl.pallas_call(land, out_shape=tuple((jax.ShapeDtypeStruct(r.shape, r.dty...]
where the time goes in v3:
time: 80.4 us; the launch traced here: 80.2 us
  Pallas kernels  79.6 us (99%)
    pallas_call x1, Pallas kernels, per_device(): pl.pallas_call(kernel, out_shape=(jax.ShapeDtypeStruct((8, d), BF16), jax...  77.4 us
    pallas_call x1, Pallas kernels, per_device(): pl.pallas_call(land, out_shape=tuple((jax.ShapeDtypeStruct(r.shape, r.dty...  2.18 us

profile of v3, /device:TPU:1, one launch (start us, length us, event | category | flops | bytes accessed | tf_op | source)
XLA Modules:
  0.0 80.2 jit_solution(15352302155583797122)
XLA Ops:
  0.6 77.4 %swiglu_exchange.1 = (bf16[8,256]{1,0:T(8,128)(2,1)}, bf16[8,256]{1,0:T(8,128)(2,1)}, bf16[256,896]{1,0:T(8,128)(2,1)}, bf16[256,896]{1,0:T(8,128)(2,1)}, bf16[896,256]{1,0:T(8,128)(2,1)}) custom-call(bf16[8,256]{1,0:T(8,128)(2,1)} %tok_hbm.1, bf16[8,256]{1,0:T(8,128)(2,1)} %grad_hbm.1, bf16[256,896]{1,0:T(8,128)(2,1)} %gw_hbm.1, bf16[256,896]{1,0:T(8,128)(2,1)} %uw_hbm.1, ...), custom_call_target="tpu_custom_call" | custom-call | tf_op jit(solution)/shard_map/swiglu_exchange/pallas_call | solution.py:331
  78.0 2.2 %land.1 = (bf16[8,256]{1,0:T(8,128)(2,1)}, bf16[8,256]{1,0:T(8,128)(2,1)}, bf16[256,896]{1,0:T(8,128)(2,1)}, bf16[256,896]{1,0:T(8,128)(2,1)}, bf16[896,256]{1,0:T(8,128)(2,1)}) custom-call(bf16[8,256]{1,0:T(8,128)(2,1)} %get-tuple-element.10.refs_0_, bf16[8,256]{1,0:T(8,128)(2,1)} %get-tuple-element.11.refs_1_, bf16[256,896]{1,0:T(8,128)(2,1)} %get-tuple-element.12.refs_2_, ...), custom_call_target="tpu_custom_call" | custom-call | tf_op jit(solution)/shard_map/land/pallas_call | solution.py:380

commit v4 on v3

--- a/solution.py
+++ b/solution.py
@@ -11,6 +11,8 @@
 BF16 = jnp.bfloat16
 FAR = (2, 1, 3)
 NEAR = (1, 3, 2)
+Z_NEAR = (12, 4, 13, 3, 14, 2, 15, 1)
+Z_FAR = (11, 5, 10, 6, 9, 7, 8)
 
 
 def dot(left, right, left_dim, right_dim):
@@ -24,10 +26,10 @@
     lo_ref, gt_ref, gg_hbm, gu_hbm, gd_hbm,
     gw, uw, dw, gath0, gath1,
     part0, part1, core_in0, core_in1, pack0, pack1, x_in0, x_in1, y_out0, y_out1, y_in0, y_in1,
-    acts0, acts1, p4, n_in, zpack, z_in, gg, gu, gd,
+    far_out0, far_out1, far_in0, far_in1, acts0, acts1, p4, n_in, zpack, z_in, gg, gu, gd,
     load_sem, store_sem,
     tz_send, tz_recv, ty_send, ty_recv,
-    sc_send, sc_recv, sx_send, sx_recv, sy_send, sy_recv,
+    sc_send, sc_recv, sx_send, sx_recv, sy_send, sy_recv, sf_send, sf_recv,
     ay_send, ay_recv, ax_send, ax_recv, ac_send, ac_recv,
     on_send, on_recv, oz_send, oz_recv,
 ):
@@ -36,6 +38,7 @@
     x, core = lax.div(depth, 2), lax.rem(depth, 2)
     d, ff = gw.shape
     gath = (gath0, gath1)
+    far_out, far_in = (far_out0, far_out1), (far_in0, far_in1)
     part, core_in, pack = (part0, part1), (core_in0, core_in1), (pack0, pack1)
     x_in, y_out, y_in, acts = (x_in0, x_in1), (y_out0, y_out1), (y_in0, y_in1), (acts0, acts1)
 
@@ -62,9 +65,6 @@
 
     def left(ref, send):
         remote(ref, ref, send, load_sem.at[0], core_dev).wait_send()
-
-    def z_off(i):
-        return 8 + lax.div(i + 1, 2) * (2 * lax.rem(i, 2) - 1)
 
     def col_at(q):
         return lax.rem(col + q, 4)
@@ -89,11 +89,8 @@
     def greet(device):
         pl.semaphore_signal(barrier, inc=1, device_id=device, device_id_type=MESH)
 
-    def greet_z(i, c):
-        greet(z_dev(lax.rem(z + z_off(i), 16)))
-        return c
-
-    lax.fori_loop(0, 15, greet_z, 0)
+    for off in Z_NEAR:
+        greet(z_dev(lax.rem(z + off, 16)))
     for step in FAR:
         greet(col_dev(col_at(step)))
         greet(x_dev(x_at(step)))
@@ -101,69 +98,81 @@
     greet(core_dev)
     for load in own_loads:
         load.wait()
-    pl.semaphore_wait(barrier, 23)
+    pl.semaphore_wait(barrier, 16)
 
     def pass_on(p, src_z):
         slot = gath[p].at[y_lo * 16 + src_z]
         remote(slot, slot, ty_send.at[p], ty_recv.at[p], next_dev).start()
 
     def gather_start(p):
-        def body(i, c):
-            slot = gath[p].at[row]
-            remote(slot, slot, tz_send.at[p], tz_recv.at[p * 16 + z], z_dev(lax.rem(z + z_off(i), 16))).start()
-            return c
-        lax.fori_loop(0, 15, body, 0)
+        slot = gath[p].at[row]
+        for off in Z_NEAR:
+            remote(
+                slot, slot, tz_send.at[p], tz_recv.at[p * 16 + z], z_dev(lax.rem(z + off, 16))
+            ).start()
         pass_on(p, z)
 
-    def gather_pass(p):
-        def body(k, c):
-            src_z = lax.rem(z + 16 - z_off(14 - k), 16)
-            arrived(gath[p].at[y_lo * 16 + src_z], tz_recv.at[p * 16 + src_z])
+    def gather_pass(p, offs):
+        for off in offs:
+            src_z = lax.rem(z + off, 16)
+            slot = gath[p].at[y_lo * 16 + src_z]
+            arrived(slot, tz_recv.at[p * 16 + src_z])
+            if off in (12, 13, 14, 15) or off in (1, 2, 3):
+                onward = 4 if off > 8 else 12
+                remote(
+                    slot, slot, tz_send.at[p], tz_recv.at[p * 16 + src_z], z_dev(lax.rem(z + onward, 16))
+                ).start()
             pass_on(p, src_z)
-            return c
-        lax.fori_loop(0, 15, body, 0)
 
     def gather_all(p):
         arrived(gath[p].at[pl.ds((1 - y_lo) * 16, 16)], ty_recv.at[p])
         return gath[p][...].astype(F32).reshape(256, d).astype(BF16)
 
-    def sums_start(p):
-        for q in FAR + (0,):
-            chips = pl.ds(col_at(q) * 4, 4)
-            remote(
-                part[p].at[chips, 1 - core], core_in[p].at[chips],
-                sc_send.at[p], sc_recv.at[p * 4 + q], core_dev,
-            ).start()
-
-    def sums_x(p, q):
-        first = col_at(q) * 4
+    def col_of(j):
+        return lax.rem(2 * y_lo + j, 4)
+
+    def sums_start(p, j):
+        chips = pl.ds(col_of(j) * 4, 4)
+        remote(
+            part[p].at[chips, 1 - core], core_in[p].at[chips],
+            sc_send.at[p], sc_recv.at[p * 4 + j], core_dev,
+        ).start()
+
+    def sums_x(p, j):
+        first = col_of(j) * 4
         chips = pl.ds(first, 4)
-        arrived(core_in[p].at[chips], sc_recv.at[p * 4 + q])
+        arrived(core_in[p].at[chips], sc_recv.at[p * 4 + j])
         pack[p][chips] = (part[p][chips, core] + core_in[p][chips]).astype(BF16)
         for step in FAR:
             remote(
                 pack[p].at[first + x_at(step)], x_in[p].at[first + x],
-                sx_send.at[p], sx_recv.at[p * 4 + col_at(q)], x_dev(x_at(step)),
+                sx_send.at[p], sx_recv.at[p * 4 + j], x_dev(x_at(step)),
             ).start()
 
-    def sums_y(p, q):
-        first = col_at(q) * 4
-        arrived(x_in[p].at[pl.ds(0, 3)], sx_recv.at[p * 4 + col_at(q)])
+    def sums_y(p, j):
+        to = col_of(j)
+        first = to * 4
+        arrived(x_in[p].at[pl.ds(0, 3)], sx_recv.at[p * 4 + j])
         total = part[p][first + x, core] + core_in[p][first + x]
         for step in FAR:
             total = total + x_in[p][first + x_at(step)].astype(F32)
-        y_out[p][col_at(q)] = total
-        if q:
-            remote(
-                y_out[p].at[col_at(q)], y_in[p].at[col], sy_send.at[p], sy_recv.at[p], col_dev(col_at(q))
-            ).start()
+        y_out[p][to] = total
+        away = lax.rem(to + 4 - col, 4)
+
+        @pl.when(away == 2)
+        def _():
+            far_out[p][...] = total.astype(BF16)
+            remote(far_out[p], far_in[p], sf_send.at[p], sf_recv.at[p], col_dev(to)).start()
+
+        @pl.when(lax.rem(away, 2) == 1)
+        def _():
+            remote(y_out[p].at[to], y_in[p].at[col], sy_send.at[p], sy_recv.at[p], col_dev(to)).start()
 
     def sums_total(p):
-        arrived(y_in[p].at[pl.ds(0, 3)], sy_recv.at[p])
-        total = y_out[p][col]
-        for q in FAR:
-            total = total + y_in[p][col_at(q)]
-        return total
+        arrived(y_in[p].at[pl.ds(0, 2)], sy_recv.at[p])
+        total = y_out[p][col] + y_in[p][col_at(1)] + y_in[p][col_at(3)]
+        arrived(far_in[p], sf_recv.at[p])
+        return total + far_in[p][...].astype(F32)
 
     def acts_x(p, q):
         slot = acts[p].at[col_at(q) * 4 + x, core]
@@ -222,32 +231,50 @@
 
     gather_start(0)
     gather_start(1)
-    gather_pass(0)
-    tok_all = gather_all(0)
+    gather_pass(0, Z_NEAR[::-1])
+    gather_pass(1, Z_NEAR[::-1])
+    gather_pass(0, Z_FAR)
     for load in loads:
         load.wait()
-    part0[:, :, :, 0:ff] = dot(tok_all, gw[...], 1, 0).reshape(16, 2, 8, ff)
-    part0[:, :, :, ff:] = dot(tok_all, uw[...], 1, 0).reshape(16, 2, 8, ff)
-    sums_start(0)
-    gather_pass(1)
-    for q in FAR + (0,):
-        sums_x(0, q)
+
+    def gate_up(half):
+        tok = gath0[pl.ds(half * 16, 16)].astype(F32).reshape(128, d).astype(BF16)
+        chips = pl.ds(half * 8, 8)
+        part0[chips, :, :, 0:ff] = dot(tok, gw[...], 1, 0).reshape(8, 2, 8, ff)
+        part0[chips, :, :, ff:] = dot(tok, uw[...], 1, 0).reshape(8, 2, 8, ff)
+
+    gate_up(y_lo)
+    sums_start(0, 0)
+    sums_start(0, 1)
+    gather_pass(1, Z_FAR)
+    sums_x(0, 0)
+    sums_x(0, 1)
+    tok_all = gather_all(0)
+    gate_up(1 - y_lo)
+    sums_start(0, 2)
+    sums_start(0, 3)
     grad_all = gather_all(1)
     part1[...] = dot(grad_all, dw[...], 1, 1).reshape(16, 2, 8, ff)
-    sums_start(1)
-    for q in FAR:
-        sums_y(0, q)
-    for q in FAR + (0,):
-        sums_x(1, q)
+    sums_x(0, 2)
+    sums_x(0, 3)
+    for j in range(4):
+        sums_start(1, j)
     sums_y(0, 0)
+    sums_y(0, 1)
+    sums_x(1, 0)
+    sums_x(1, 1)
+    sums_y(0, 2)
+    sums_x(1, 2)
+    sums_x(1, 3)
+    sums_y(0, 3)
     total = sums_total(0)
     gate_pre = total[:, 0:ff]
     up_proj = total[:, ff:]
     sig = jax.nn.sigmoid(gate_pre)
     acts0[col * 4 + x, core] = (gate_pre * sig * up_proj).astype(BF16)
     acts_start(0)
-    for q in FAR + (0,):
-        sums_y(1, q)
+    for j in range(4):
+        sums_y(1, j)
     for q in NEAR:
         acts_y(0, q)
     d_hidden = sums_total(1)
@@ -261,23 +288,35 @@
     for q in NEAR:
         acts_y(1, q)
     acts_all(0)
+    def out_terms(p, half):
+        rows = acts[p][pl.ds(half * 8, 8)].astype(F32)
+        if p == 0:
+            term = dot(rows.reshape(128, ff).astype(BF16), dw[...], 1, 0)
+        else:
+            term = dot(rows[:, :, :, 0:ff].reshape(128, ff).astype(BF16), gw[...], 1, 1) + dot(
+                rows[:, :, :, ff:].reshape(128, ff).astype(BF16), uw[...], 1, 1
+            )
+        p4[p, half] = term.reshape(16, 8, d)
+
+    out_terms(0, 1 - y_lo)
+    out_start(0)
+    out_terms(0, y_lo)
     hid = acts0[...].astype(F32).reshape(256, ff).astype(BF16)
-    p4[0] = dot(hid, dw[...], 1, 0).reshape(2, 16, 8, d)
-    out_start(0)
     for q in (0,) + NEAR:
         acts_core(1, q)
     for q in FAR + (0,):
         out_z(0, q)
     acts_all(1)
+    out_terms(1, 1 - y_lo)
+    out_start(1)
+    out_terms(1, y_lo)
     d_gate = acts1[:, :, :, 0:ff].astype(F32).reshape(256, ff).astype(BF16)
     d_up = acts1[:, :, :, ff:].astype(F32).reshape(256, ff).astype(BF16)
-    p4[1] = (dot(d_gate, gw[...], 1, 1) + dot(d_up, uw[...], 1, 1)).reshape(2, 16, 8, d)
-    out_start(1)
+    for q in FAR + (0,):
+        out_z(1, q)
     gg[...] = dot(tok_all, d_gate, 0, 0).astype(BF16)
     stores = [pltpu.make_async_copy(gg, gg_hbm, store_sem.at[0])]
     stores[0].start()
-    for q in FAR + (0,):
-        out_z(1, q)
     gu[...] = dot(tok_all, d_up, 0, 0).astype(BF16)
     stores.append(pltpu.make_async_copy(gu, gu_hbm, store_sem.at[1]))
     stores[1].start()
@@ -289,7 +328,8 @@
         left(gath[p].at[pl.ds(0, 16)], ty_send.at[p])
         left(core_in[p], sc_send.at[p])
         left(pack[p].at[pl.ds(0, 12)], sx_send.at[p])
-        left(y_in[p].at[pl.ds(0, 3)], sy_send.at[p])
+        left(y_in[p].at[pl.ds(0, 2)], sy_send.at[p])
+        left(far_in[p], sf_send.at[p])
         left(acts[p].at[pl.ds(0, 3), core], ay_send.at[p])
         left(acts[p].at[pl.ds(0, 12), core], ax_send.at[p])
         left(acts[p].at[:, core], ac_send.at[p])
@@ -327,7 +367,6 @@
     vmem = pl.BlockSpec(memory_space=pltpu.VMEM)
     hbm = pl.BlockSpec(memory_space=pltpu.HBM)
     dma = pltpu.SemaphoreType.DMA
-    pair = (1, 1)
     results = pl.pallas_call(
         kernel,
         out_shape=(
@@ -357,6 +396,10 @@
             pltpu.VMEM((4, 8, ff), F32),
             pltpu.VMEM((4, 8, 2 * ff), F32),
             pltpu.VMEM((4, 8, ff), F32),
+            pltpu.VMEM((8, 2 * ff), BF16),
+            pltpu.VMEM((8, ff), BF16),
+            pltpu.VMEM((8, 2 * ff), BF16),
+            pltpu.VMEM((8, ff), BF16),
             pltpu.VMEM((16, 2, 8, ff), BF16),
             pltpu.VMEM((16, 2, 8, 2 * ff), BF16),
             pltpu.VMEM((2, 2, 16, 8, d), F32),
@@ -368,7 +411,7 @@
             pltpu.VMEM((ff, d), BF16),
             dma((5,)), dma((3,)),
             dma((2,)), dma((32,)), dma((2,)), dma((2,)),
-            dma((2,)), dma((8,)), dma((2,)), dma((8,)), dma((2,)), dma((2,)),
+            dma((2,)), dma((8,)), dma((2,)), dma((8,)), dma((2,)), dma((2,)), dma((2,)), dma((2,)),
             dma((2,)), dma((8,)), dma((2,)), dma((8,)), dma((2,)), dma((2,)),
             dma((2,)), dma((8,)), dma((2,)), dma((2,)),
         ],

time: 80.4 us -> 77.8 us (0.968)
  Pallas kernels: 79.6 us -> 77 us
    pallas_call x1, Pallas kernels: 77.4 us -> 74.8 us  [per_device(): pl.pallas_call(kernel, out_shape=(jax.ShapeDtypeStruct((8, d), BF16), jax...]
where the time goes in v4:
time: 77.8 us; the launch traced here: 77.6 us
  Pallas kernels  77 us (99%)
    pallas_call x1, Pallas kernels, per_device(): pl.pallas_call(kernel, out_shape=(jax.ShapeDtypeStruct((8, d), BF16), jax...  74.8 us
    pallas_call x1, Pallas kernels, per_device(): pl.pallas_call(land, out_shape=tuple((jax.ShapeDtypeStruct(r.shape, r.dty...  2.18 us

profile of v4, /device:TPU:1, one launch (start us, length us, event | category | flops | bytes accessed | tf_op | source)
XLA Modules:
  0.0 77.6 jit_solution(11495587580000568168)
XLA Ops:
  0.6 74.8 %swiglu_exchange.1 = (bf16[8,256]{1,0:T(8,128)(2,1)}, bf16[8,256]{1,0:T(8,128)(2,1)}, bf16[256,896]{1,0:T(8,128)(2,1)}, bf16[256,896]{1,0:T(8,128)(2,1)}, bf16[896,256]{1,0:T(8,128)(2,1)}) custom-call(bf16[8,256]{1,0:T(8,128)(2,1)} %tok_hbm.1, bf16[8,256]{1,0:T(8,128)(2,1)} %grad_hbm.1, bf16[256,896]{1,0:T(8,128)(2,1)} %gw_hbm.1, bf16[256,896]{1,0:T(8,128)(2,1)} %uw_hbm.1, ...), custom_call_target="tpu_custom_call" | custom-call | tf_op jit(solution)/shard_map/swiglu_exchange/pallas_call | solution.py:370
  75.4 2.2 %land.1 = (bf16[8,256]{1,0:T(8,128)(2,1)}, bf16[8,256]{1,0:T(8,128)(2,1)}, bf16[256,896]{1,0:T(8,128)(2,1)}, bf16[256,896]{1,0:T(8,128)(2,1)}, bf16[896,256]{1,0:T(8,128)(2,1)}) custom-call(bf16[8,256]{1,0:T(8,128)(2,1)} %get-tuple-element.10.refs_0_, bf16[8,256]{1,0:T(8,128)(2,1)} %get-tuple-element.11.refs_1_, bf16[256,896]{1,0:T(8,128)(2,1)} %get-tuple-element.12.refs_2_, ...), custom_call_target="tpu_custom_call" | custom-call | tf_op jit(solution)/shard_map/land/pallas_call | solution.py:423

commit v5 on v4

--- a/solution.py
+++ b/solution.py
@@ -128,18 +128,24 @@
         arrived(gath[p].at[pl.ds((1 - y_lo) * 16, 16)], ty_recv.at[p])
         return gath[p][...].astype(F32).reshape(256, d).astype(BF16)
 
-    def col_of(j):
-        return lax.rem(2 * y_lo + j, 4)
+    def col_of(p, j):
+        if p:
+            return col_at((FAR + (0,))[j])
+        half = lax.rem(y_lo + j // 2, 2)
+        apart = half - lax.div(col, 2)
+        odd = lax.rem(col, 2)
+        first = odd + (1 - apart * apart) * (1 - 2 * odd)
+        return 2 * half + (first if j % 2 == 0 else 1 - first)
 
     def sums_start(p, j):
-        chips = pl.ds(col_of(j) * 4, 4)
+        chips = pl.ds(col_of(p, j) * 4, 4)
         remote(
             part[p].at[chips, 1 - core], core_in[p].at[chips],
             sc_send.at[p], sc_recv.at[p * 4 + j], core_dev,
         ).start()
 
     def sums_x(p, j):
-        first = col_of(j) * 4
+        first = col_of(p, j) * 4
         chips = pl.ds(first, 4)
         arrived(core_in[p].at[chips], sc_recv.at[p * 4 + j])
         pack[p][chips] = (part[p][chips, core] + core_in[p][chips]).astype(BF16)
@@ -150,7 +156,7 @@
             ).start()
 
     def sums_y(p, j):
-        to = col_of(j)
+        to = col_of(p, j)
         first = to * 4
         arrived(x_in[p].at[pl.ds(0, 3)], sx_recv.at[p * 4 + j])
         total = part[p][first + x, core] + core_in[p][first + x]
@@ -249,24 +255,20 @@
     gather_pass(1, Z_FAR)
     sums_x(0, 0)
     sums_x(0, 1)
-    tok_all = gather_all(0)
+    arrived(gath0.at[pl.ds((1 - y_lo) * 16, 16)], ty_recv.at[0])
     gate_up(1 - y_lo)
     sums_start(0, 2)
     sums_start(0, 3)
+    sums_x(0, 2)
+    sums_x(0, 3)
     grad_all = gather_all(1)
     part1[...] = dot(grad_all, dw[...], 1, 1).reshape(16, 2, 8, ff)
-    sums_x(0, 2)
-    sums_x(0, 3)
     for j in range(4):
         sums_start(1, j)
-    sums_y(0, 0)
-    sums_y(0, 1)
-    sums_x(1, 0)
-    sums_x(1, 1)
-    sums_y(0, 2)
-    sums_x(1, 2)
-    sums_x(1, 3)
-    sums_y(0, 3)
+    for j in range(4):
+        sums_y(0, j)
+    for j in range(4):
+        sums_x(1, j)
     total = sums_total(0)
     gate_pre = total[:, 0:ff]
     up_proj = total[:, ff:]
@@ -300,10 +302,10 @@
 
     out_terms(0, 1 - y_lo)
     out_start(0)
+    for q in (0, 1, 3):
+        acts_core(1, q)
     out_terms(0, y_lo)
-    hid = acts0[...].astype(F32).reshape(256, ff).astype(BF16)
-    for q in (0,) + NEAR:
-        acts_core(1, q)
+    acts_core(1, 2)
     for q in FAR + (0,):
         out_z(0, q)
     acts_all(1)
@@ -314,6 +316,8 @@
     d_up = acts1[:, :, :, ff:].astype(F32).reshape(256, ff).astype(BF16)
     for q in FAR + (0,):
         out_z(1, q)
+    hid = acts0[...].astype(F32).reshape(256, ff).astype(BF16)
+    tok_all = gath0[...].astype(F32).reshape(256, d).astype(BF16)
     gg[...] = dot(tok_all, d_gate, 0, 0).astype(BF16)
     stores = [pltpu.make_async_copy(gg, gg_hbm, store_sem.at[0])]
     stores[0].start()

time: 77.8 us -> 76.7 us (0.986)
  Pallas kernels: 77 us -> 75.9 us
    pallas_call x1, Pallas kernels: 74.8 us -> 73.7 us  [per_device(): pl.pallas_call(kernel, out_shape=(jax.ShapeDtypeStruct((8, d), BF16), jax...]
where the time goes in v5:
time: 76.7 us; the launch traced here: 76.5 us
  Pallas kernels  75.9 us (99%)
    pallas_call x1, Pallas kernels, per_device(): pl.pallas_call(kernel, out_shape=(jax.ShapeDtypeStruct((8, d), BF16), jax...  73.7 us
    pallas_call x1, Pallas kernels, per_device(): pl.pallas_call(land, out_shape=tuple((jax.ShapeDtypeStruct(r.shape, r.dty...  2.18 us

profile of v5, /device:TPU:1, one launch (start us, length us, event | category | flops | bytes accessed | tf_op | source)
XLA Modules:
  0.0 76.5 jit_solution(12959879254080104812)
XLA Ops:
  0.6 73.7 %swiglu_exchange.1 = (bf16[8,256]{1,0:T(8,128)(2,1)}, bf16[8,256]{1,0:T(8,128)(2,1)}, bf16[256,896]{1,0:T(8,128)(2,1)}, bf16[256,896]{1,0:T(8,128)(2,1)}, bf16[896,256]{1,0:T(8,128)(2,1)}) custom-call(bf16[8,256]{1,0:T(8,128)(2,1)} %tok_hbm.1, bf16[8,256]{1,0:T(8,128)(2,1)} %grad_hbm.1, bf16[256,896]{1,0:T(8,128)(2,1)} %gw_hbm.1, bf16[256,896]{1,0:T(8,128)(2,1)} %uw_hbm.1, ...), custom_call_target="tpu_custom_call" | custom-call | tf_op jit(solution)/shard_map/swiglu_exchange/pallas_call | solution.py:374
  74.4 2.2 %land.1 = (bf16[8,256]{1,0:T(8,128)(2,1)}, bf16[8,256]{1,0:T(8,128)(2,1)}, bf16[256,896]{1,0:T(8,128)(2,1)}, bf16[256,896]{1,0:T(8,128)(2,1)}, bf16[896,256]{1,0:T(8,128)(2,1)}) custom-call(bf16[8,256]{1,0:T(8,128)(2,1)} %get-tuple-element.10.refs_0_, bf16[8,256]{1,0:T(8,128)(2,1)} %get-tuple-element.11.refs_1_, bf16[256,896]{1,0:T(8,128)(2,1)} %get-tuple-element.12.refs_2_, ...), custom_call_target="tpu_custom_call" | custom-call | tf_op jit(solution)/shard_map/land/pallas_call | solution.py:427

commit v6 on v5

--- a/solution.py
+++ b/solution.py
@@ -240,6 +240,7 @@
     gather_pass(0, Z_NEAR[::-1])
     gather_pass(1, Z_NEAR[::-1])
     gather_pass(0, Z_FAR)
+    gather_pass(1, Z_FAR)
     for load in loads:
         load.wait()
 
@@ -252,7 +253,6 @@
     gate_up(y_lo)
     sums_start(0, 0)
     sums_start(0, 1)
-    gather_pass(1, Z_FAR)
     sums_x(0, 0)
     sums_x(0, 1)
     arrived(gath0.at[pl.ds((1 - y_lo) * 16, 16)], ty_recv.at[0])

time: 76.7 us -> 76.9 us (level)
  no operation moved by 1% of the time
where the time goes in v6:
time: 76.9 us; the launch traced here: 76.7 us
  Pallas kernels  76 us (99%)
    pallas_call x1, Pallas kernels, per_device(): pl.pallas_call(kernel, out_shape=(jax.ShapeDtypeStruct((8, d), BF16), jax...  73.8 us
    pallas_call x1, Pallas kernels, per_device(): pl.pallas_call(land, out_shape=tuple((jax.ShapeDtypeStruct(r.shape, r.dty...  2.18 us

profile of v6, /device:TPU:1, one launch (start us, length us, event | category | flops | bytes accessed | tf_op | source)
XLA Modules:
  0.0 76.7 jit_solution(17557579776399235928)
XLA Ops:
  0.6 73.8 %swiglu_exchange.1 = (bf16[8,256]{1,0:T(8,128)(2,1)}, bf16[8,256]{1,0:T(8,128)(2,1)}, bf16[256,896]{1,0:T(8,128)(2,1)}, bf16[256,896]{1,0:T(8,128)(2,1)}, bf16[896,256]{1,0:T(8,128)(2,1)}) custom-call(bf16[8,256]{1,0:T(8,128)(2,1)} %tok_hbm.1, bf16[8,256]{1,0:T(8,128)(2,1)} %grad_hbm.1, bf16[256,896]{1,0:T(8,128)(2,1)} %gw_hbm.1, bf16[256,896]{1,0:T(8,128)(2,1)} %uw_hbm.1, ...), custom_call_target="tpu_custom_call" | custom-call | tf_op jit(solution)/shard_map/swiglu_exchange/pallas_call | solution.py:374
  74.5 2.2 %land.1 = (bf16[8,256]{1,0:T(8,128)(2,1)}, bf16[8,256]{1,0:T(8,128)(2,1)}, bf16[256,896]{1,0:T(8,128)(2,1)}, bf16[256,896]{1,0:T(8,128)(2,1)}, bf16[896,256]{1,0:T(8,128)(2,1)}) custom-call(bf16[8,256]{1,0:T(8,128)(2,1)} %get-tuple-element.10.refs_0_, bf16[8,256]{1,0:T(8,128)(2,1)} %get-tuple-element.11.refs_1_, bf16[256,896]{1,0:T(8,128)(2,1)} %get-tuple-element.12.refs_2_, ...), custom_call_target="tpu_custom_call" | custom-call | tf_op jit(solution)/shard_map/land/pallas_call | solution.py:427
